TPU v7x, 32 devices: a whole 2x2x4 slice. The times are simulated.
32 devices in a mesh: groups: 2 (over y), wide: 16 (over z, x, core).
Axes of the slice: x: 2, y: 2, z: 4, core: 2. Of those that a mesh axis runs over, the one named last changes fastest.
Arguments:
- queries: bfloat16 [2048, 768], P(('groups', 'wide')), parts along dimension 0, may hold values from -6 to 6
- beam_owner: int32 [2048, 4], P(('groups', 'wide')), parts along dimension 0, may hold values from 0 to 15, all different within a row; in each aligned block of 64 rows (0 to 63, 64 to 127, ...) at most 32 rows name the same one
- beam_local: int32 [2048, 8], P(('groups', 'wide')), parts along dimension 0, may hold values from 0 to 127
- leaf_weight: bfloat16 [4096, 16, 768], P(('groups', 'wide')), parts along dimension 0, may hold values from -0.4375 to 0.4375
- leaf_bias: float32 [4096, 16], P(('groups', 'wide')), parts along dimension 0, may hold values from -2 to 2
- cluster_weight: bfloat16 [4096, 768], P(('groups', 'wide')), parts along dimension 0, may hold values from -0.4375 to 0.4375
- block_size: int32 [4096], P(('groups', 'wide')), parts along dimension 0, may hold values from 1 to 16
Outputs:
- label_scores: float32 [2048, 128], P(('groups', 'wide')), parts along dimension 0
There are 2 independent parts, one for each index of `groups`. A program takes and returns all parts, laid end to end along the dimension named above; each array names one. Nothing has to cross between parts.
Inputs may be any that keep to these rules, and one draw needn't show every extreme that they name: `beam_owner`: each query names 4 different devices. Among the rows of one device no device is named more than 32 times, and some device is named exactly 32 times.
All inputs are finite; a program needn't handle non-finite values.
Results may differ from a plain program's by a relative error of at most 0.0003.
Values may be sent and summed in bfloat16 or wider, within the bound.
A program may use at most 64 MiB of HBM per device.

v0:
```python
import jax
import jax.numpy as jnp
from jax import lax
from jax.sharding import PartitionSpec as P


def slot_numbers(destination, devices, capacity):
    dest_hits = (destination[:, None] == jnp.arange(devices, dtype=jnp.int32)[None, :]).astype(
        jnp.int32
    )
    before = jnp.sum(jnp.cumsum(dest_hits, axis=0) * dest_hits, axis=1) - 1
    return destination * capacity + before


def finish_scores(parent, leaf_logit, safe_ids, leaf_bias, block_size):
    label_width = leaf_logit.shape[2]
    leaf_logit = leaf_logit + jnp.take(leaf_bias, safe_ids, axis=0)
    inside = (
        jnp.arange(label_width, dtype=jnp.int32)[None, None, :]
        < jnp.take(block_size, safe_ids, axis=0)[:, :, None]
    )
    scored = jnp.where(inside, jax.nn.sigmoid(parent)[:, :, None] * jax.nn.sigmoid(leaf_logit), 0.0)
    return scored.reshape(parent.shape[0], -1)


def score_block(row_data, clusters, leaf_weight, leaf_bias, cluster_weight, block_size):
    occupied = clusters >= 0
    safe_ids = jnp.where(occupied, clusters, 0)
    blocks = jnp.take(leaf_weight, safe_ids, axis=0)
    vectors = jnp.take(cluster_weight, safe_ids, axis=0)
    leaf_logit = jnp.einsum("sd,sgjd->sgj", row_data, blocks, preferred_element_type=jnp.float32)
    parent = jnp.einsum("sd,sgd->sg", row_data, vectors, preferred_element_type=jnp.float32)
    return finish_scores(parent, leaf_logit, safe_ids, leaf_bias, block_size)


def score_slots(row_data, clusters, leaf_weight, leaf_bias, cluster_weight, block_size):
    slot_total = row_data.shape[0]
    group_size = clusters.shape[1]
    block_rows = 256
    padded = -(-slot_total // block_rows) * block_rows
    label_width = leaf_weight.shape[1]
    out_width = group_size * label_width

    def score_packed(packed):
        return score_block(packed[0], packed[1], leaf_weight, leaf_bias, cluster_weight, block_size)

    stacked = lax.map(
        score_packed,
        (
            row_data.reshape(padded // block_rows, block_rows, -1),
            clusters.reshape(padded // block_rows, block_rows, group_size),
        ),
    )
    result = stacked.reshape(padded, out_width)
    return result


def on_device(queries, beam_owner, beam_local, leaf_weight, leaf_bias, cluster_weight, block_size):
    devices = lax.axis_size("wide")
    query_count = queries.shape[0]
    owner_count = beam_owner.shape[1]
    beam_count = beam_local.shape[1]
    features = queries.shape[1]
    label_width = leaf_weight.shape[1]
    capacity = 2 * query_count * owner_count // devices
    destination = jnp.repeat(beam_owner, 2, axis=1).reshape(-1)
    slot_room = 2 * capacity
    slot_index = slot_numbers(destination, devices, slot_room)
    source = jnp.arange(query_count * beam_count, dtype=jnp.int32) // beam_count
    outgoing = (
        jnp.zeros((devices * slot_room, features), queries.dtype)
        .at[slot_index]
        .set(jnp.take(queries, source, axis=0))
    )
    wanted = (
        jnp.full((devices * slot_room, 1), -1, jnp.int32)
        .at[slot_index]
        .set(beam_local.reshape(-1, 1))
    )
    rows_in = lax.all_to_all(
        outgoing.reshape(devices, slot_room, features),
        "wide",
        split_axis=0,
        concat_axis=0,
        tiled=True,
    )
    ids_in = lax.all_to_all(
        wanted.reshape(devices, slot_room, 1), "wide", split_axis=0, concat_axis=0, tiled=True
    )
    senders = ids_in.shape[0]
    slot_count = ids_in.shape[1]
    scored = score_slots(
        rows_in.reshape(senders * slot_count, features),
        ids_in.reshape(senders * slot_count, 1),
        leaf_weight,
        leaf_bias,
        cluster_weight,
        block_size,
    )
    returned = lax.all_to_all(
        scored.reshape(senders, slot_count, label_width),
        "wide",
        split_axis=0,
        concat_axis=0,
        tiled=True,
    )
    gathered_back = returned.reshape(devices * slot_room, -1)
    return jnp.take(gathered_back, slot_index, axis=0).reshape(
        query_count, beam_count * label_width
    )


def solution(mesh):
    return jax.shard_map(
        on_device,
        mesh=mesh,
        in_specs=(
            P(("groups", "wide"), None),
            P(("groups", "wide"), None),
            P(("groups", "wide"), None),
            P(("groups", "wide"), None, None),
            P(("groups", "wide"), None),
            P(("groups", "wide"), None),
            P(("groups", "wide")),
        ),
        out_specs=P(("groups", "wide"), None),
        check_vma=False,
    )
```

profile of v0, /device:TPU:0, one launch (start us, length us, event | category | flops | bytes accessed | tf_op | source)
XLA Modules:
  0.0 161.3 jit_solution(17737549912113906396)
XLA Ops:
  0.0 0.9 copy.33
  0.9 0.8 broadcast_in_dim.89
  1.7 1.1 eq.26
  2.8 1.1 reshape_reshape.12
  3.8 0.7 broadcast_multiply_fusion
  4.5 1.1 reduce-window.6
  5.7 0.2 slice_reduce_fusion
  5.9 0.1 fusion.13
  6.1 0.8 broadcast_in_dim.88
  6.9 1.1 mul.44
  8.0 0.8 copy.36
  8.8 2.4 %scatter_custom_fusion = s32[1024]{0:T(1024)S(1)} fusion(s32[512]{0:T(512)S(1)} %bitcast.64, s32[512]{0:T(512)S(1)} %reshape.323, s32[]{:T(128)} %constant.125.clone.1), kind=kCustom, calls=%fused_computation.59 | custom fusion | bytes 4100 | tf_op jit(solution)/shard_map/scatter | solution.py:78
  11.3 0.7 reshape.266
  12.0 7.4 %all-to-all-start = ((s32[16,64,1]{1,2,0:T(1,128)}), s32[16,64,1]{1,2,0:T(1,128)S(1)}, u32[]{:S(2)}, u32[]{:S(2)}) async-start(s32[16,64,1]{1,2,0:T(1,128)} %reshape.266), calls=%async_computation | async-start | bytes 16384 | tf_op jit(solution)/shard_map/all_to_all | solution.py:87
  19.4 6.8 %scatter_custom_fusion.1 = bf16[1024,768]{1,0:T(8,128)(2,1)} fusion(s32[512]{0:T(512)S(1)} %bitcast.65, bf16[]{:T(256)} %constant.129.clone.1, pred[512]{0:T(512)(128)(4,1)S(1)} %compare_and_fusion.2, bf16[]{:T(256)} %constant.134.clone.1, bf16[64,768]{1,0:T(8,128)(2,1)S(1)} %copy-done, s32[1024]{0:T(1024)S(1)} %pad_clamp_fusion.2), kind=kCustom, calls=%fused_computation.28 | custom fusion | flops 393216 | bytes 1675780 | tf_op jit(solution)/shard_map/scatter | solution.py:73
  26.2 6.1 %all-to-all-start.1 = ((bf16[16,64,768]{2,1,0:T(8,128)(2,1)}), bf16[16,64,768]{2,1,0:T(8,128)(2,1)}, u32[]{:S(2)}, u32[]{:S(2)}) async-start(bf16[16,64,768]{2,1,0:T(8,128)(2,1)} %bitcast.55), calls=%async_computation.1 | async-start | bytes 3145728 | tf_op jit(solution)/shard_map/all_to_all | solution.py:80
  32.4 0.8 copy.38
  33.2 0.7 copy.35
  33.8 0.5 broadcast.393
  34.3 0.6 reduce.7
  35.0 29.3 %all-to-all-done.1 = bf16[16,64,768]{2,1,0:T(8,128)(2,1)} async-done(((bf16[16,64,768]{2,1,0:T(8,128)(2,1)}), bf16[16,64,768]{2,1,0:T(8,128)(2,1)}, u32[]{:S(2)}, u32[]{:S(2)}) %all-to-all-start.1) | async-done | bytes 1572896 | tf_op jit(solution)/shard_map/all_to_all | solution.py:80
  64.3 75.4 %while.10 = (s32[]{:T(128)}, f32[4,256,16]{2,1,0:T(8,128)}, s32[4,256,1]{1,2,0:T(1,128)S(1)}, s32[128]{0:T(128)S(1)}, bf16[4,256,768]{2,1,0:T(8,128)(2,1)}, /*in...) while((s32[]{:T(128)}, f32[4,256,16]{2,1,0:T(8,128)}, ...), condition=%wide.region_6.7_spmd, body=%wide.region_5.6_spmd.sunk | while | flops 10458114 | bytes 22093416 | solution.py:47
  64.4 1.9 %gather_fusion.1 = s32[256]{0:T(256)S(1)} fusion(s32[128]{0:T(128)S(1)} %get-tuple-element.178, s32[1024]{0:T(1024)S(1)} %pad_clamp_fusion.4), kind=kCustom, calls=%fused_computation.clone.1 | custom fusion | bytes 3072 | tf_op jit(solution)/shard_map/while/body/eval_jaxpr/jit(_take)/gather | solution.py:20
  66.3 3.6 %gather_fusion = bf16[256,16,768]{2,1,0:T(8,128)(2,1)} fusion(bf16[128,16,768]{2,1,0:T(8,128)(2,1)S(1)} %get-tuple-element.181, s32[1024]{0:T(1024)S(1)} %pad_clamp_fusion.4), kind=kCustom, calls=%fused_computation.2.clone.1 | custom fusion | bytes 12583936 | tf_op jit(solution)/shard_map/while/body/eval_jaxpr/jit(_take)/gather | solution.py:29
  69.9 1.0 dynamic-slice_bitcast_fusion.2
  70.9 5.8 %fusion.27 = f32[256,1,16]{2,1,0:T(1,128)} fusion(bf16[256,16,768]{2,1,0:T(8,128)(2,1)} %gather_fusion, pred[256]{0:T(512)(128)(4,1)S(1)} %get-tuple-element.155, bf16[256,768,1]{1,0,2:T(8,128)(2,1)S(1)} %dynamic-slice_bitcast_fusion.2), kind=kOutput, calls=%fused_computation.8.clone.1 | convolution fusion | flops 9437184 | bytes 6701312 | tf_op jit(solution)/shard_map/while/body/eval_jaxpr/sd,sgjd->sgj/dot_general | solution.py:31
  76.8 1.9 %gather_fusion.3 = bf16[256,768]{1,0:T(8,128)(2,1)} fusion(bf16[128,768]{1,0:T(8,128)(2,1)S(1)} %get-tuple-element.180, s32[1024]{0:T(1024)S(1)} %pad_clamp_fusion.4), kind=kCustom, calls=%fused_computation.1.clone.1 | custom fusion | bytes 787456 | tf_op jit(solution)/shard_map/while/body/eval_jaxpr/jit(_take)/gather | solution.py:30
  78.7 1.4 fusion.28
  80.1 1.3 gather_fusion.2
  81.4 1.8 %bitcast_dynamic-update-slice_fusion.2 = f32[4,256,16]{2,1,0:T(8,128)} fusion(f32[4,256,16]{2,1,0:T(8,128)} %get-tuple-element.167, s32[]{:T(128)} %get-tuple-element.166, f32[256,16]{1,0:T(8,128)} %bitcast.56, f32[256,16]{1,0:T(8,128)} %gather_fusion.2, f32[256]{0:T(256)S(1)} %add_divide_fusion.2, s32[256]{0:T(256)S(1)} %get-tuple-element.156, ...), kind=kLoop, calls=%fused_computation.16.clone.1 | loop fusion | flops 32768 | bytes 396032 | tf_op jit(solution)/shard_map/while/body/jit(dynamic_update_index_in_dim)/dynamic_update_slice | solution.py:47
  83.2 1.9 %gather_fusion.1 = s32[256]{0:T(256)S(1)} fusion(s32[128]{0:T(128)S(1)} %get-tuple-element.178, s32[1024]{0:T(1024)S(1)} %pad_clamp_fusion.4), kind=kCustom, calls=%fused_computation.clone.1 | custom fusion | bytes 3072 | tf_op jit(solution)/shard_map/while/body/eval_jaxpr/jit(_take)/gather | solution.py:20
  85.1 3.6 %gather_fusion = bf16[256,16,768]{2,1,0:T(8,128)(2,1)} fusion(bf16[128,16,768]{2,1,0:T(8,128)(2,1)S(1)} %get-tuple-element.181, s32[1024]{0:T(1024)S(1)} %pad_clamp_fusion.4), kind=kCustom, calls=%fused_computation.2.clone.1 | custom fusion | bytes 12583936 | tf_op jit(solution)/shard_map/while/body/eval_jaxpr/jit(_take)/gather | solution.py:29
  88.7 1.0 dynamic-slice_bitcast_fusion.2
  89.8 5.8 %fusion.27 = f32[256,1,16]{2,1,0:T(1,128)} fusion(bf16[256,16,768]{2,1,0:T(8,128)(2,1)} %gather_fusion, pred[256]{0:T(512)(128)(4,1)S(1)} %get-tuple-element.155, bf16[256,768,1]{1,0,2:T(8,128)(2,1)S(1)} %dynamic-slice_bitcast_fusion.2), kind=kOutput, calls=%fused_computation.8.clone.1 | convolution fusion | flops 9437184 | bytes 6701312 | tf_op jit(solution)/shard_map/while/body/eval_jaxpr/sd,sgjd->sgj/dot_general | solution.py:31
  95.6 1.9 %gather_fusion.3 = bf16[256,768]{1,0:T(8,128)(2,1)} fusion(bf16[128,768]{1,0:T(8,128)(2,1)S(1)} %get-tuple-element.180, s32[1024]{0:T(1024)S(1)} %pad_clamp_fusion.4), kind=kCustom, calls=%fused_computation.1.clone.1 | custom fusion | bytes 787456 | tf_op jit(solution)/shard_map/while/body/eval_jaxpr/jit(_take)/gather | solution.py:30
  97.5 1.4 fusion.28
  98.9 1.3 gather_fusion.2
  100.3 1.8 %bitcast_dynamic-update-slice_fusion.2 = f32[4,256,16]{2,1,0:T(8,128)} fusion(f32[4,256,16]{2,1,0:T(8,128)} %get-tuple-element.167, s32[]{:T(128)} %get-tuple-element.166, f32[256,16]{1,0:T(8,128)} %bitcast.56, f32[256,16]{1,0:T(8,128)} %gather_fusion.2, f32[256]{0:T(256)S(1)} %add_divide_fusion.2, s32[256]{0:T(256)S(1)} %get-tuple-element.156, ...), kind=kLoop, calls=%fused_computation.16.clone.1 | loop fusion | flops 32768 | bytes 396032 | tf_op jit(solution)/shard_map/while/body/jit(dynamic_update_index_in_dim)/dynamic_update_slice | solution.py:47
  102.1 1.9 %gather_fusion.1 = s32[256]{0:T(256)S(1)} fusion(s32[128]{0:T(128)S(1)} %get-tuple-element.178, s32[1024]{0:T(1024)S(1)} %pad_clamp_fusion.4), kind=kCustom, calls=%fused_computation.clone.1 | custom fusion | bytes 3072 | tf_op jit(solution)/shard_map/while/body/eval_jaxpr/jit(_take)/gather | solution.py:20
  104.0 3.6 %gather_fusion = bf16[256,16,768]{2,1,0:T(8,128)(2,1)} fusion(bf16[128,16,768]{2,1,0:T(8,128)(2,1)S(1)} %get-tuple-element.181, s32[1024]{0:T(1024)S(1)} %pad_clamp_fusion.4), kind=kCustom, calls=%fused_computation.2.clone.1 | custom fusion | bytes 12583936 | tf_op jit(solution)/shard_map/while/body/eval_jaxpr/jit(_take)/gather | solution.py:29
  107.6 1.0 dynamic-slice_bitcast_fusion.2
  108.6 5.8 %fusion.27 = f32[256,1,16]{2,1,0:T(1,128)} fusion(bf16[256,16,768]{2,1,0:T(8,128)(2,1)} %gather_fusion, pred[256]{0:T(512)(128)(4,1)S(1)} %get-tuple-element.155, bf16[256,768,1]{1,0,2:T(8,128)(2,1)S(1)} %dynamic-slice_bitcast_fusion.2), kind=kOutput, calls=%fused_computation.8.clone.1 | convolution fusion | flops 9437184 | bytes 6701312 | tf_op jit(solution)/shard_map/while/body/eval_jaxpr/sd,sgjd->sgj/dot_general | solution.py:31
  114.4 1.9 %gather_fusion.3 = bf16[256,768]{1,0:T(8,128)(2,1)} fusion(bf16[128,768]{1,0:T(8,128)(2,1)S(1)} %get-tuple-element.180, s32[1024]{0:T(1024)S(1)} %pad_clamp_fusion.4), kind=kCustom, calls=%fused_computation.1.clone.1 | custom fusion | bytes 787456 | tf_op jit(solution)/shard_map/while/body/eval_jaxpr/jit(_take)/gather | solution.py:30
  116.4 1.4 fusion.28
  117.8 1.3 gather_fusion.2
  119.1 1.8 %bitcast_dynamic-update-slice_fusion.2 = f32[4,256,16]{2,1,0:T(8,128)} fusion(f32[4,256,16]{2,1,0:T(8,128)} %get-tuple-element.167, s32[]{:T(128)} %get-tuple-element.166, f32[256,16]{1,0:T(8,128)} %bitcast.56, f32[256,16]{1,0:T(8,128)} %gather_fusion.2, f32[256]{0:T(256)S(1)} %add_divide_fusion.2, s32[256]{0:T(256)S(1)} %get-tuple-element.156, ...), kind=kLoop, calls=%fused_computation.16.clone.1 | loop fusion | flops 32768 | bytes 396032 | tf_op jit(solution)/shard_map/while/body/jit(dynamic_update_index_in_dim)/dynamic_update_slice | solution.py:47
  120.9 1.9 %gather_fusion.1 = s32[256]{0:T(256)S(1)} fusion(s32[128]{0:T(128)S(1)} %get-tuple-element.178, s32[1024]{0:T(1024)S(1)} %pad_clamp_fusion.4), kind=kCustom, calls=%fused_computation.clone.1 | custom fusion | bytes 3072 | tf_op jit(solution)/shard_map/while/body/eval_jaxpr/jit(_take)/gather | solution.py:20
  122.8 3.6 %gather_fusion = bf16[256,16,768]{2,1,0:T(8,128)(2,1)} fusion(bf16[128,16,768]{2,1,0:T(8,128)(2,1)S(1)} %get-tuple-element.181, s32[1024]{0:T(1024)S(1)} %pad_clamp_fusion.4), kind=kCustom, calls=%fused_computation.2.clone.1 | custom fusion | bytes 12583936 | tf_op jit(solution)/shard_map/while/body/eval_jaxpr/jit(_take)/gather | solution.py:29
  126.4 1.0 dynamic-slice_bitcast_fusion.2
  127.4 5.8 %fusion.27 = f32[256,1,16]{2,1,0:T(1,128)} fusion(bf16[256,16,768]{2,1,0:T(8,128)(2,1)} %gather_fusion, pred[256]{0:T(512)(128)(4,1)S(1)} %get-tuple-element.155, bf16[256,768,1]{1,0,2:T(8,128)(2,1)S(1)} %dynamic-slice_bitcast_fusion.2), kind=kOutput, calls=%fused_computation.8.clone.1 | convolution fusion | flops 9437184 | bytes 6701312 | tf_op jit(solution)/shard_map/while/body/eval_jaxpr/sd,sgjd->sgj/dot_general | solution.py:31
  133.3 1.9 %gather_fusion.3 = bf16[256,768]{1,0:T(8,128)(2,1)} fusion(bf16[128,768]{1,0:T(8,128)(2,1)S(1)} %get-tuple-element.180, s32[1024]{0:T(1024)S(1)} %pad_clamp_fusion.4), kind=kCustom, calls=%fused_computation.1.clone.1 | custom fusion | bytes 787456 | tf_op jit(solution)/shard_map/while/body/eval_jaxpr/jit(_take)/gather | solution.py:30
  135.2 1.4 fusion.28
  136.6 1.3 gather_fusion.2
  137.9 1.8 %bitcast_dynamic-update-slice_fusion.2 = f32[4,256,16]{2,1,0:T(8,128)} fusion(f32[4,256,16]{2,1,0:T(8,128)} %get-tuple-element.167, s32[]{:T(128)} %get-tuple-element.166, f32[256,16]{1,0:T(8,128)} %bitcast.56, f32[256,16]{1,0:T(8,128)} %gather_fusion.2, f32[256]{0:T(256)S(1)} %add_divide_fusion.2, s32[256]{0:T(256)S(1)} %get-tuple-element.156, ...), kind=kLoop, calls=%fused_computation.16.clone.1 | loop fusion | flops 32768 | bytes 396032 | tf_op jit(solution)/shard_map/while/body/jit(dynamic_update_index_in_dim)/dynamic_update_slice | solution.py:47
  139.8 1.2 copy.40
  141.0 0.8 reshape.368
  141.7 9.1 %all-to-all-start.2 = ((f32[16,1,1024]{2,1,0:T(1,128)}), f32[16,1,1024]{2,1,0:T(1,128)S(1)}, u32[]{:S(2)}, u32[]{:S(2)}) async-start(f32[16,1,1024]{2,1,0:T(1,128)} %reshape.368), calls=%async_computation.2 | async-start | bytes 131072 | tf_op jit(solution)/shard_map/all_to_all | solution.py:100
  150.9 6.8 %all-to-all-done.2 = f32[16,1,1024]{2,1,0:T(1,128)S(1)} async-done(((f32[16,1,1024]{2,1,0:T(1,128)}), f32[16,1,1024]{2,1,0:T(1,128)S(1)}, u32[]{:S(2)}, u32[]{:S(2)}) %all-to-all-start.2) | async-done | bytes 65568 | tf_op jit(solution)/shard_map/all_to_all | solution.py:100
  157.7 0.5 broadcast.396
  158.3 0.8 reduce.8
  159.1 0.2 copy.41
  159.4 1.0 gather_fusion.4
  160.4 0.1 gather.36
  160.6 0.7 copy.43
  (50 shorter events, 0.8 us)
Async XLA Ops:
  0.0 19.4 %copy-start = (bf16[64,768]{1,0:T(8,128)(2,1)S(1)}, bf16[64,768]{1,0:T(8,128)(2,1)}, u32[]{:S(2)}) copy-start(bf16[64,768]{1,0:T(8,128)(2,1)} %param.9) | copy-start | bytes 294916
  0.0 64.3 %copy-start.3 = (bf16[128,16,768]{2,1,0:T(8,128)(2,1)S(1)}, bf16[128,16,768]{2,1,0:T(8,128)(2,1)}, u32[]{:S(2)}) copy-start(bf16[128,16,768]{2,1,0:T(8,128)(2,1)} %param.12) | copy-start | bytes 9437188
  0.0 64.3 %copy-start.2 = (bf16[128,768]{1,0:T(8,128)(2,1)S(1)}, bf16[128,768]{1,0:T(8,128)(2,1)}, u32[]{:S(2)}) copy-start(bf16[128,768]{1,0:T(8,128)(2,1)} %param.14) | copy-start | bytes 589828
  0.0 64.3 %copy-start.1 = (s32[128]{0:T(128)S(1)}, s32[128]{0:T(128)}, u32[]{:S(2)}) copy-start(s32[128]{0:T(128)} %param.15) | copy-start | bytes 1540
  8.8 23.5 %copy-start.5 = (s32[512,1]{0,1:T(1,128)}, s32[512,1]{0,1:T(1,128)S(1)}, u32[]{:S(2)}) copy-start(s32[512,1]{0,1:T(1,128)S(1)} %compare_select_fusion.5) | copy-start | bytes 6148
  12.0 14.2 %all-to-all-start = ((s32[16,64,1]{1,2,0:T(1,128)}), s32[16,64,1]{1,2,0:T(1,128)S(1)}, u32[]{:S(2)}, u32[]{:S(2)}) async-start(s32[16,64,1]{1,2,0:T(1,128)} %reshape.266), calls=%async_computation | async-start | bytes 16384 | tf_op jit(solution)/shard_map/all_to_all | solution.py:87
  26.2 38.1 %all-to-all-start.1 = ((bf16[16,64,768]{2,1,0:T(8,128)(2,1)}), bf16[16,64,768]{2,1,0:T(8,128)(2,1)}, u32[]{:S(2)}, u32[]{:S(2)}) async-start(bf16[16,64,768]{2,1,0:T(8,128)(2,1)} %bitcast.55), calls=%async_computation.1 | async-start | bytes 3145728 | tf_op jit(solution)/shard_map/all_to_all | solution.py:80
  64.3 86.5 %copy-start.4 = (s32[64,8]{0,1:T(8,128)S(1)}, s32[64,8]{0,1:T(8,128)}, u32[]{:S(2)}) copy-start(s32[64,8]{0,1:T(8,128)} %copy.35) | copy-start | bytes 6148
  64.3 86.6 %copy-start.6 = (s32[512,1]{0,1:T(1,128)S(1)}, s32[512,1]{0,1:T(1,128)}, u32[]{:S(2)}) copy-start(s32[512,1]{0,1:T(1,128)} %copy-done.5) | copy-start | bytes 6148
  141.7 16.0 %all-to-all-start.2 = ((f32[16,1,1024]{2,1,0:T(1,128)}), f32[16,1,1024]{2,1,0:T(1,128)S(1)}, u32[]{:S(2)}, u32[]{:S(2)}) async-start(f32[16,1,1024]{2,1,0:T(1,128)} %reshape.368), calls=%async_computation.2 | async-start | bytes 131072 | tf_op jit(solution)/shard_map/all_to_all | solution.py:100
where the time goes:
time: 162 us; the launch traced here: 161 us
  local copies, waits for them, and re-layouts  55.9 us (35%)
  waiting for transfers between devices  36.1 us (22%)
  matrix products  23.4 us (14%)
  other arithmetic  23.1 us (14%)
  starting transfers between devices  22.5 us (14%)
    all_to_all x1, waiting for transfers between devices, on_device(): lax.all_to_all(outgoing.reshape(devices, slot_room, features), 'wide', sp...  29.3 us
    dot_general x4, matrix products, score_block(): jnp.einsum('sd,sgjd->sgj', row_data, blocks, preferred_element_type=jnp.f...  23.4 us
    gather x4, local copies, waits for them, and re-layouts, score_block(): blocks = jnp.take(leaf_weight, safe_ids, axis=0)  14.5 us
    all_to_all x1, starting transfers between devices, on_device(): lax.all_to_all(scored.reshape(senders, slot_count, label_width), 'wide',...  9.11 us
    gather x4, local copies, waits for them, and re-layouts, score_block(): vectors = jnp.take(cluster_weight, safe_ids, axis=0)  7.69 us
    gather x4, local copies, waits for them, and re-layouts, finish_scores(): jnp.take(block_size, safe_ids, axis=0)[:, :, None]  7.47 us
    all_to_all x1, starting transfers between devices, on_device(): lax.all_to_all(wanted.reshape(devices, slot_room, 1), 'wide', split_axis=...  7.37 us
    dynamic_update_slice x4, other arithmetic, score_slots(): lax.map(score_packed, (row_data.reshape(padded // block_rows, block_rows,...  7.14 us
  transfers between devices with their start and end apart: 3, of which 2 were waited for; matrix products, arithmetic and copies ran while one was open for 6% of the time, Pallas kernels for 0%

commit v1 on v0

v1 whole, which is shorter than its diff:
```python
import functools

import jax
import jax.numpy as jnp
from jax import lax
from jax.experimental import pallas as pl
from jax.experimental.pallas import tpu as pltpu
from jax.sharding import PartitionSpec as P

MESH = pl.DeviceIdType.MESH
NT = (((1,), (1,)), ((), ()))
QUAD = 4
SMALL = 16


def loop(count, body):
    if count <= SMALL:
        for step in range(count):
            body(step)
    else:
        lax.fori_loop(0, count, lambda step, carry: (body(step), carry)[1], 0)


def chips_along_x(devices):
    x = 1
    while 8 * x * x <= devices // 2:
        x *= 2
    return x


def kernel(
    n, nx, slots,
    q_hbm, owner_ref, local_ref, w_hbm, bias_ref, cw_hbm, size_ref,
    out_ref,
    gath, idx, w, cw, xc, stage, ret, pick,
    send_q, send_i, recv_q, recv_i, send_r, recv_r, own_sem, w_sem, cw_sem,
):
    rows, features = q_hbm.shape
    clusters = cw_hbm.shape[0]
    labels = w_hbm.shape[0] // clusters
    pair = 2 * labels
    nz = n // (2 * nx)
    quads_per_plane = nx // 2
    me = lax.axis_index("wide")
    core = lax.rem(me, 2)
    x = lax.rem(me // 2, nx)
    z = me // (2 * nx)

    def index_of(z_, x_, core_):
        return (z_ * nx + x_) * 2 + core_

    def plane(k):
        return lax.rem(z + k, nz)

    barrier = pltpu.get_barrier_semaphore()

    def greet(step):
        pl.semaphore_signal(
            barrier, inc=1, device_id={"wide": lax.rem(me + step + 1, n)}, device_id_type=MESH
        )

    loop(n - 1, greet)

    own_copy = pltpu.make_async_copy(q_hbm, gath.at[me], own_sem)
    own_copy.start()
    w_copy = pltpu.make_async_copy(w_hbm, w, w_sem)
    w_copy.start()
    cw_copy = pltpu.make_async_copy(cw_hbm, cw, cw_sem)
    cw_copy.start()

    owner = owner_ref[...]
    local = local_ref[...]
    named = jnp.concatenate(
        [owner[k // 2:k // 2 + 1] * clusters + local[k:k + 1] for k in range(local.shape[0])], axis=0
    )
    idx[me] = jnp.concatenate([named, named], axis=1)

    pl.semaphore_wait(barrier, n - 1)

    def send_chunk(source, number, slot, target):
        pltpu.make_async_remote_copy(
            src_ref=idx.at[number], dst_ref=idx.at[number],
            send_sem=send_i.at[slot], recv_sem=recv_i.at[number],
            device_id={"wide": target}, device_id_type=MESH,
        ).start()
        pltpu.make_async_remote_copy(
            src_ref=source, dst_ref=gath.at[number],
            send_sem=send_q.at[slot], recv_sem=recv_q.at[number],
            device_id={"wide": target}, device_id_type=MESH,
        ).start()

    def wait_chunk(number):
        pltpu.make_async_copy(idx.at[number], idx.at[number], recv_i.at[number]).wait()
        pltpu.make_async_copy(gath.at[number], gath.at[number], recv_q.at[number]).wait()

    def to_column(step):
        send_chunk(q_hbm, me, step, index_of(lax.rem(z + nz - 1 - step, nz), x, core))

    x_base = nz - 1
    c_base = x_base + nz * (nx - 1)

    def to_row(source, number, k):
        def one(step):
            other = lax.rem(x + 1 + step, nx)
            send_chunk(source, number, x_base + k * (nx - 1) + step, index_of(z, other, core))
        loop(nx - 1, one)

    def to_sibling(source, number, k, step):
        send_chunk(source, number, c_base + k * nx + step, index_of(z, x, 1 - core))

    to_row(q_hbm, me, 0)
    loop(nz - 1, to_column)
    to_sibling(q_hbm, me, 0, 0)

    def from_column(k):
        number = index_of(plane(k), x, core)
        wait_chunk(number)
        to_row(gath.at[number], number, k)
        to_sibling(gath.at[number], number, k, 0)

    def from_row(k):
        def one(step):
            number = index_of(plane(k), lax.rem(x + 1 + step, nx), core)
            wait_chunk(number)
            to_sibling(gath.at[number], number, k, 1 + step)
        loop(nx - 1, one)

    def from_sibling(k):
        def one(step):
            wait_chunk(index_of(plane(k), step, 1 - core))
        loop(nx, one)

    def prepare_pick():
        dev = lax.broadcasted_iota(jnp.int32, (n, rows), 0)
        hits = [owner[k:k + 1] == dev for k in range(owner.shape[0])]
        any_hit = functools.reduce(jnp.logical_or, hits)
        before = (
            lax.broadcasted_iota(jnp.int32, (rows, rows), 0)
            < lax.broadcasted_iota(jnp.int32, (rows, rows), 1)
        )
        rank = jnp.dot(
            any_hit.astype(jnp.bfloat16), before.astype(jnp.bfloat16),
            preferred_element_type=jnp.float32,
        )
        places = [
            jnp.sum(jnp.where(hit, rank, 0.0), axis=0, keepdims=True)
            + (owner[k:k + 1] * slots).astype(jnp.float32)
            for k, hit in enumerate(hits)
        ]
        place = jnp.concatenate(places + [jnp.zeros((8 - len(places), rows), jnp.float32)], axis=0)
        place = jnp.concatenate([place, jnp.zeros((8, 128 - rows), jnp.float32)], axis=1)
        place = place.T.astype(jnp.int32)
        lane = lax.broadcasted_iota(jnp.int32, (rows, n * slots), 1)
        for k in range(owner.shape[0]):
            pick[k] = (place[:rows, k:k + 1] == lane).astype(jnp.bfloat16)

    bias = bias_ref[...]
    hi = bias.astype(jnp.bfloat16)
    rest = bias - hi.astype(jnp.float32)
    mid = rest.astype(jnp.bfloat16)
    low = (rest - mid.astype(jnp.float32)).astype(jnp.bfloat16)
    size = jnp.broadcast_to(size_ref[...].astype(jnp.float32), (labels, clusters)).astype(jnp.bfloat16)
    table = jnp.concatenate([hi, mid, low, size], axis=0)

    width = QUAD * rows

    def quad_number(position):
        return plane(position // quads_per_plane) * quads_per_plane + position % quads_per_plane

    def compact(position, half, slot_of):
        first = QUAD * quad_number(position)
        lane = lax.broadcasted_iota(jnp.int32, (8, 128), 1)
        row = lax.broadcasted_iota(jnp.int32, (8, 128), 0)
        parts = []
        for p in range(QUAD // 2):
            ids = jnp.where(lane < rows, idx[first + 2 * p], idx[first + 2 * p + 1])
            ids = ids - me * clusters
            inside = (ids >= 0) & (ids < clusters)
            value = jnp.where(inside, ids, 0).astype(jnp.float32)
            even = row % 2 == 0
            c0 = jnp.sum(jnp.where(even, value, 0.0), axis=0, keepdims=True)
            c1 = jnp.sum(jnp.where(even, 0.0, value), axis=0, keepdims=True)
            hit = jnp.sum(jnp.where(even & inside, 1.0, 0.0), axis=0, keepdims=True)
            parts.append((c0, c1, hit))
        c0, c1, hit = [jnp.concatenate(v, axis=1) for v in zip(*parts)]
        qa = lax.broadcasted_iota(jnp.int32, (width, width), 0)
        qb = lax.broadcasted_iota(jnp.int32, (width, width), 1)
        before = ((qa < qb) & (qa // rows == qb // rows)).astype(jnp.bfloat16)
        rank = jnp.dot(
            jnp.broadcast_to(hit, (8, width)).astype(jnp.bfloat16), before,
            preferred_element_type=jnp.float32,
        )[:1].astype(jnp.int32)
        lane = lax.broadcasted_iota(jnp.int32, (1, width), 1)
        place = jnp.where(hit > 0.5, rank + lane // rows * slots, -1)
        taken = (
            place == lax.broadcasted_iota(jnp.int32, (QUAD * slots, width), 0)
        ).astype(jnp.bfloat16)
        row = lax.broadcasted_iota(jnp.int32, (8, width), 0)
        both = jnp.where(row == 0, c0, jnp.where(row == 1, c1, 0.0)).astype(jnp.bfloat16)
        chosen = lax.dot_general(both, taken, NT, preferred_element_type=jnp.float32)
        embedded = gath[pl.ds(first, QUAD)].reshape(width, features)
        packed = jnp.dot(taken, embedded, preferred_element_type=jnp.float32)
        xc[slot_of, half * QUAD * slots:(half + 1) * QUAD * slots] = packed.astype(jnp.bfloat16)
        return chosen[0:1], chosen[1:2]

    def score(batch, slot_of):
        chosen = [compact(2 * batch + half, half, slot_of) for half in range(2)]
        ids = [jnp.concatenate(v, axis=1).astype(jnp.int32) for v in zip(*chosen)]
        lanes = 2 * QUAD * slots
        x_rows = xc[slot_of]
        wide_ids = [jnp.broadcast_to(v, (labels, lanes)) for v in ids]
        logit = [jnp.zeros((labels, lanes), jnp.float32) for _ in ids]
        step = min(16, clusters)
        for start in range(0, clusters, step):
            block = lax.dot_general(
                w[start * labels:(start + step) * labels], x_rows, NT,
                preferred_element_type=jnp.float32,
            )
            for c in range(step):
                piece = block[c * labels:(c + 1) * labels]
                logit = [jnp.where(v == start + c, piece, a) for v, a in zip(wide_ids, logit)]
        product = lax.dot_general(cw[...], x_rows, NT, preferred_element_type=jnp.float32)
        number = lax.broadcasted_iota(jnp.int32, (clusters, lanes), 0)
        scores = []
        for v, a in zip(ids, logit):
            hot = number == v
            parent = jnp.sum(jnp.where(hot, product, 0.0), axis=0, keepdims=True)
            extra = jnp.dot(table, hot.astype(jnp.bfloat16), preferred_element_type=jnp.float32)
            b = extra[:labels] + extra[labels:2 * labels] + extra[2 * labels:3 * labels]
            used = extra[3 * labels:]
            slot = lax.broadcasted_iota(jnp.int32, (labels, lanes), 0).astype(jnp.float32)
            value = jax.nn.sigmoid(parent) * jax.nn.sigmoid(a + b)
            scores.append(jnp.where(slot < used, value, 0.0))
        scores = jnp.concatenate(scores, axis=0)
        lane = lax.broadcasted_iota(jnp.int32, (8, 128), 1)
        for half in range(2):
            first = QUAD * quad_number(2 * batch + half)
            for t in range(QUAD):
                tile = jnp.zeros((8, 128), jnp.float32)
                for g in range(QUAD):
                    part = scores[8 * g:8 * g + 8, half * 128:half * 128 + 128]
                    shift = (slots * (g - t)) % 128
                    if shift:
                        part = pltpu.roll(part, shift, axis=1)
                    tile = jnp.where(lane // slots == g, part, tile)
                stage[first + t] = tile
        for half in range(2):
            first = QUAD * quad_number(2 * batch + half)
            for t in range(QUAD):
                target = first + t

                @pl.when(target != me)
                def _():
                    pltpu.make_async_remote_copy(
                        src_ref=stage.at[target], dst_ref=ret.at[me],
                        send_sem=send_r.at[target], recv_sem=recv_r.at[me],
                        device_id={"wide": target}, device_id_type=MESH,
                    ).start()

                @pl.when(target == me)
                def _():
                    ret[me] = stage[me]

    batches = n // (2 * QUAD)
    if n <= SMALL and nx == 2:
        own_copy.wait()
        for k in range(1, nz):
            from_column(k)
            from_row(k - 1)
            if k == 1:
                prepare_pick()
                w_copy.wait()
                cw_copy.wait()
        from_sibling(0)
        from_sibling(1)
        score(0, 0)
        from_row(nz - 1)
        from_sibling(2)
        from_sibling(3)
        score(1, 1)
    else:
        prepare_pick()
        own_copy.wait()
        from_row(0)

        def relay(step):
            from_column(step + 1)
            from_row(step + 1)

        loop(nz - 1, relay)
        loop(nz, from_sibling)
        w_copy.wait()
        cw_copy.wait()
        lax.fori_loop(0, batches, lambda b, carry: (score(b, 0), carry)[1], 0)

    def wait_return(step):
        source = lax.rem(me + 1 + step, n)
        pltpu.make_async_copy(ret.at[source], ret.at[source], recv_r.at[source]).wait()

    loop(n - 1, wait_return)

    lane = lax.broadcasted_iota(jnp.int32, (8, 128), 1)
    columns = []
    for d in range(0, n, QUAD):
        tiles = [ret[d + t] for t in range(QUAD)]
        parts = []
        for g in range(QUAD):
            part = jnp.zeros((8, 128), jnp.float32)
            for t in range(QUAD):
                shift = (slots * (t - g)) % 128
                moved = pltpu.roll(tiles[t], shift, axis=1) if shift else tiles[t]
                part = jnp.where(lane // slots == t, moved, part)
            parts.append(part)
        columns.append(jnp.concatenate(parts, axis=0))
    back = jnp.concatenate(columns, axis=1)
    head = back.astype(jnp.bfloat16)
    tail = (back - head.astype(jnp.float32)).astype(jnp.bfloat16)
    result = jnp.zeros(out_ref.shape, jnp.float32)
    owners = owner.shape[0]
    for term in (head, tail):
        for k in range(owners):
            spread = jnp.concatenate(
                [term if j == k else jnp.zeros_like(term) for j in range(owners)], axis=0
            )
            result += lax.dot_general(pick[k], spread, NT, preferred_element_type=jnp.float32)
    out_ref[...] = result

    def wait_sent(step):
        pltpu.make_async_copy(idx.at[0], idx.at[0], send_i.at[step]).wait()
        pltpu.make_async_copy(gath.at[0], gath.at[0], send_q.at[step]).wait()

    def wait_returned(step):
        target = lax.rem(me + 1 + step, n)
        pltpu.make_async_copy(stage.at[target], stage.at[target], send_r.at[target]).wait()

    loop(n - 1, wait_sent)
    loop(n - 1, wait_returned)


def on_device(n, queries, beam_owner, beam_local, leaf_weight, leaf_bias, cluster_weight, block_size):
    rows, features = queries.shape
    owners = beam_owner.shape[1]
    clusters, labels, _ = leaf_weight.shape
    slots = max(32, 2 * rows * owners // n)
    assert slots == 32 and rows == 64 and 2 * labels * owners == 128 and n % 8 == 0
    vmem = pl.BlockSpec(memory_space=pltpu.VMEM)
    hbm = pl.BlockSpec(memory_space=pl.ANY)
    dma = pltpu.SemaphoreType.DMA
    return pl.pallas_call(
        functools.partial(kernel, n, chips_along_x(n), slots),
        out_shape=jax.ShapeDtypeStruct((rows, 2 * labels * owners), jnp.float32),
        in_specs=[hbm, vmem, vmem, hbm, vmem, hbm, vmem],
        out_specs=vmem,
        scratch_shapes=[
            pltpu.VMEM((n, rows, features), queries.dtype),
            pltpu.VMEM((n, 8, 128), jnp.int32),
            pltpu.VMEM((clusters * labels, features), leaf_weight.dtype),
            pltpu.VMEM((clusters, features), cluster_weight.dtype),
            pltpu.VMEM((2, 2 * QUAD * slots, features), jnp.bfloat16),
            pltpu.VMEM((n, 8, 128), jnp.float32),
            pltpu.VMEM((n, 8, 128), jnp.float32),
            pltpu.VMEM((owners, rows, n * slots), jnp.bfloat16),
            dma((n - 1,)), dma((n - 1,)), dma((n,)), dma((n,)), dma((n,)), dma((n,)),
            dma, dma, dma,
        ],
        compiler_params=pltpu.CompilerParams(
            collective_id=0, has_side_effects=True, vmem_limit_bytes=48 * 2**20
        ),
    )(
        queries,
        beam_owner.T,
        beam_local.T,
        leaf_weight.reshape(clusters * labels, features),
        leaf_bias.T,
        cluster_weight,
        block_size.reshape(1, clusters),
    )


def solution(mesh):
    spec = P(("groups", "wide"))
    return jax.shard_map(
        functools.partial(on_device, mesh.shape["wide"]),
        mesh=mesh,
        in_specs=(spec,) * 7,
        out_specs=spec,
        check_vma=False,
    )
```

time: 162 us -> 36.4 us (0.22)
  local copies, waits for them, and re-layouts: 55.9 us -> 7.04 us
  waiting for transfers between devices: 36.1 us -> 0 us
  Pallas kernels: 0 us -> 29 us
  matrix products: 23.4 us -> 0 us
  other arithmetic: 23.1 us -> 0 us
  starting transfers between devices: 22.5 us -> 0 us
    gather x19 -> x0, local copies, waits for them, and re-layouts: 36.2 us -> none  [the longest x4 14.5 us: score_block(): blocks = jnp.take(leaf_weight, safe_ids, axis=0)]
    all_to_all x3 -> x0, waiting for transfers between devices: 36.1 us -> none  [the longest x1 29.3 us: on_device(): lax.all_to_all(outgoing.reshape(devices, slot_room, features), 'wide', sp...]
    pallas_call x0 -> x1, Pallas kernels: none -> 29 us  [on_device(): pl.pallas_call(functools.partial(kernel, n, chips_along_x(n), slots), out...]
    dot_general x4 -> x0, matrix products: 23.4 us -> none  [score_block(): jnp.einsum('sd,sgjd->sgj', row_data, blocks, preferred_element_type=jnp.f...]
    all_to_all x3 -> x0, starting transfers between devices: 22.5 us -> none  [the longest x1 9.11 us: on_device(): lax.all_to_all(scored.reshape(senders, slot_count, label_width), 'wide',...]
    dynamic_update_slice x4 -> x0, other arithmetic: 7.14 us -> none  [score_slots(): lax.map(score_packed, (row_data.reshape(padded // block_rows, block_rows,...]
    scatter x1 -> x0, other arithmetic: 6.8 us -> none  [on_device(): outgoing = jnp.zeros((devices * slot_room, features), queries.dtype).at[s...]
    dot_general x4 -> x0, other arithmetic: 5.59 us -> none  [score_block(): jnp.einsum('sd,sgd->sg', row_data, vectors, preferred_element_type=jnp.fl...]
  transfers between devices with their start and end apart: 3 -> 0, of which waited for: 2 -> 0; matrix products, arithmetic and copies ran while one was open for 6% -> 0% of each run, Pallas kernels for 0% -> 0%
where the time goes in v1:
time: 36.4 us; the launch traced here: 36.1 us
  Pallas kernels  29 us (80%)
  local copies, waits for them, and re-layouts  7.04 us (19%)
    pallas_call x1, Pallas kernels, on_device(): pl.pallas_call(functools.partial(kernel, n, chips_along_x(n), slots), out...  29 us
    unnamed x15, local copies, waits for them, and re-layouts  7.04 us

profile of v1, /device:TPU:0, one launch (start us, length us, event | category | flops | bytes accessed | tf_op | source)
XLA Modules:
  0.0 36.1 jit_solution(3939851780360726595)
XLA Ops:
  0.0 0.0 copy-start
  0.0 1.9 %copy-done = bf16[128,16,768]{2,1,0:T(8,128)(2,1)S(1)} copy-done((bf16[128,16,768]{2,1,0:T(8,128)(2,1)S(1)}, bf16[128,16,768]{2,1,0:T(8,128)(2,1)}, u32[]{:S(2)}) %copy-start) | copy-done | bytes 3145752
  1.9 0.0 copy-start.1
  1.9 0.9 %copy-done.1 = bf16[128,768]{1,0:T(8,128)(2,1)S(1)} copy-done((bf16[128,768]{1,0:T(8,128)(2,1)S(1)}, bf16[128,768]{1,0:T(8,128)(2,1)}, u32[]{:S(2)}) %copy-start.1) | copy-done | bytes 196632
  2.8 0.0 copy-start.2
  2.8 0.9 %copy-done.2 = bf16[64,768]{1,0:T(8,128)(2,1)S(1)} copy-done((bf16[64,768]{1,0:T(8,128)(2,1)S(1)}, bf16[64,768]{1,0:T(8,128)(2,1)}, u32[]{:S(2)}) %copy-start.2) | copy-done | bytes 98328
  3.7 0.0 copy-start.3
  3.7 0.7 %copy-done.3 = f32[128,16]{0,1:T(8,128)S(1)} copy-done((f32[128,16]{0,1:T(8,128)S(1)}, f32[128,16]{0,1:T(8,128)}, u32[]{:S(2)}) %copy-start.3) | copy-done | bytes 8216
  4.4 0.0 copy-start.4
  4.4 0.7 %copy-done.4 = s32[64,8]{0,1:T(8,128)S(1)} copy-done((s32[64,8]{0,1:T(8,128)S(1)}, s32[64,8]{0,1:T(8,128)}, u32[]{:S(2)}) %copy-start.4) | copy-done | bytes 2072
  5.1 0.0 copy-start.5
  5.1 0.7 %copy-done.5 = s32[64,4]{0,1:T(4,128)S(1)} copy-done((s32[64,4]{0,1:T(4,128)S(1)}, s32[64,4]{0,1:T(4,128)}, u32[]{:S(2)}) %copy-start.5) | copy-done | bytes 1048
  5.8 0.0 copy-start.6
  5.8 0.7 %copy-done.6 = s32[128]{0:T(128)S(1)} copy-done((s32[128]{0:T(128)S(1)}, s32[128]{0:T(128)}, u32[]{:S(2)}) %copy-start.6) | copy-done | bytes 536
  6.4 29.0 %shard_map.73 = f32[64,128]{1,0:T(8,128)S(1)} custom-call(bf16[64,768]{1,0:T(8,128)(2,1)S(1)} %copy-done.2, s32[4,64]{1,0:T(4,128)S(1)} %bitcast.8, s32[8,64]{1,0:T(8,128)S(1)} %bitcast.7, bf16[2048,768]{1,0:T(8,128)(2,1)S(1)} %bitcast.5, f32[16,128]{1,0:T(8,128)S(1)} %bitcast.6, bf16[128,768]{1,0:T(8,128)(2,1)S(1)} %copy-done.1, s32[1,128]{1,0:T(1,128)S(1)} %bitcast.9), custom_call_target="tpu_custom_call" | custom-call | tf_op jit(solution)/shard_map/pallas_call | solution.py:349
  35.5 0.6 %copy.9 = f32[64,128]{1,0:T(8,128)} copy(f32[64,128]{1,0:T(8,128)S(1)} %shard_map.73) | data formatting | bytes 65536
Async XLA Ops:
  0.0 1.9 %copy-start = (bf16[128,16,768]{2,1,0:T(8,128)(2,1)S(1)}, bf16[128,16,768]{2,1,0:T(8,128)(2,1)}, u32[]{:S(2)}) copy-start(bf16[128,16,768]{2,1,0:T(8,128)(2,1)} %param.10) | copy-start | bytes 9437188
  1.9 0.9 %copy-start.1 = (bf16[128,768]{1,0:T(8,128)(2,1)S(1)}, bf16[128,768]{1,0:T(8,128)(2,1)}, u32[]{:S(2)}) copy-start(bf16[128,768]{1,0:T(8,128)(2,1)} %cw_hbm.1) | copy-start | bytes 589828
  2.8 0.9 %copy-start.2 = (bf16[64,768]{1,0:T(8,128)(2,1)S(1)}, bf16[64,768]{1,0:T(8,128)(2,1)}, u32[]{:S(2)}) copy-start(bf16[64,768]{1,0:T(8,128)(2,1)} %q_hbm.1) | copy-start | bytes 294916
  3.7 0.7 %copy-start.3 = (f32[128,16]{0,1:T(8,128)S(1)}, f32[128,16]{0,1:T(8,128)}, u32[]{:S(2)}) copy-start(f32[128,16]{0,1:T(8,128)} %param.11) | copy-start | bytes 24580
  4.4 0.7 %copy-start.4 = (s32[64,8]{0,1:T(8,128)S(1)}, s32[64,8]{0,1:T(8,128)}, u32[]{:S(2)}) copy-start(s32[64,8]{0,1:T(8,128)} %param.9) | copy-start | bytes 6148
  5.1 0.7 %copy-start.5 = (s32[64,4]{0,1:T(4,128)S(1)}, s32[64,4]{0,1:T(4,128)}, u32[]{:S(2)}) copy-start(s32[64,4]{0,1:T(4,128)} %param.8) | copy-start | bytes 3076
  5.8 0.7 %copy-start.6 = (s32[128]{0:T(128)S(1)}, s32[128]{0:T(128)}, u32[]{:S(2)}) copy-start(s32[128]{0:T(128)} %param.13) | copy-start | bytes 1540

commit v2 on v1

--- a/solution.py
+++ b/solution.py
@@ -30,10 +30,10 @@
 
 def kernel(
     n, nx, slots,
-    q_hbm, owner_ref, local_ref, w_hbm, bias_ref, cw_hbm, size_ref,
+    q_hbm, owner_hbm, local_hbm, w_hbm, bias_hbm, cw_hbm, size_hbm,
     out_ref,
-    gath, idx, w, cw, xc, stage, ret, pick,
-    send_q, send_i, recv_q, recv_i, send_r, recv_r, own_sem, w_sem, cw_sem,
+    gath, idx, w, cw, xc, stage, ret, pick, owner_ref, local_ref, bias_ref, size_ref, table,
+    send_q, send_i, recv_q, recv_i, send_r, recv_r, load_sem,
 ):
     rows, features = q_hbm.shape
     clusters = cw_hbm.shape[0]
@@ -61,12 +61,18 @@
 
     loop(n - 1, greet)
 
-    own_copy = pltpu.make_async_copy(q_hbm, gath.at[me], own_sem)
-    own_copy.start()
-    w_copy = pltpu.make_async_copy(w_hbm, w, w_sem)
-    w_copy.start()
-    cw_copy = pltpu.make_async_copy(cw_hbm, cw, cw_sem)
-    cw_copy.start()
+    loads = [
+        pltpu.make_async_copy(source, target, load_sem.at[i])
+        for i, (source, target) in enumerate([
+            (owner_hbm, owner_ref), (local_hbm, local_ref), (q_hbm, gath.at[me]),
+            (size_hbm, size_ref), (bias_hbm, bias_ref), (cw_hbm, cw), (w_hbm, w),
+        ])
+    ]
+    for load in loads:
+        load.start()
+    owner_copy, local_copy, own_copy, size_copy, bias_copy, cw_copy, w_copy = loads
+    owner_copy.wait()
+    local_copy.wait()
 
     owner = owner_ref[...]
     local = local_ref[...]
@@ -129,6 +135,17 @@
         def one(step):
             wait_chunk(index_of(plane(k), step, 1 - core))
         loop(nx, one)
+
+    def make_table():
+        size_copy.wait()
+        bias_copy.wait()
+        bias = bias_ref[...]
+        hi = bias.astype(jnp.bfloat16)
+        rest = bias - hi.astype(jnp.float32)
+        mid = rest.astype(jnp.bfloat16)
+        low = (rest - mid.astype(jnp.float32)).astype(jnp.bfloat16)
+        size = jnp.broadcast_to(size_ref[...].astype(jnp.float32), (labels, clusters))
+        table[...] = jnp.concatenate([hi, mid, low, size.astype(jnp.bfloat16)], axis=0)
 
     def prepare_pick():
         dev = lax.broadcasted_iota(jnp.int32, (n, rows), 0)
@@ -153,14 +170,6 @@
         lane = lax.broadcasted_iota(jnp.int32, (rows, n * slots), 1)
         for k in range(owner.shape[0]):
             pick[k] = (place[:rows, k:k + 1] == lane).astype(jnp.bfloat16)
-
-    bias = bias_ref[...]
-    hi = bias.astype(jnp.bfloat16)
-    rest = bias - hi.astype(jnp.float32)
-    mid = rest.astype(jnp.bfloat16)
-    low = (rest - mid.astype(jnp.float32)).astype(jnp.bfloat16)
-    size = jnp.broadcast_to(size_ref[...].astype(jnp.float32), (labels, clusters)).astype(jnp.bfloat16)
-    table = jnp.concatenate([hi, mid, low, size], axis=0)
 
     width = QUAD * rows
 
@@ -225,7 +234,7 @@
         for v, a in zip(ids, logit):
             hot = number == v
             parent = jnp.sum(jnp.where(hot, product, 0.0), axis=0, keepdims=True)
-            extra = jnp.dot(table, hot.astype(jnp.bfloat16), preferred_element_type=jnp.float32)
+            extra = jnp.dot(table[...], hot.astype(jnp.bfloat16), preferred_element_type=jnp.float32)
             b = extra[:labels] + extra[labels:2 * labels] + extra[2 * labels:3 * labels]
             used = extra[3 * labels:]
             slot = lax.broadcasted_iota(jnp.int32, (labels, lanes), 0).astype(jnp.float32)
@@ -269,6 +278,7 @@
             from_row(k - 1)
             if k == 1:
                 prepare_pick()
+                make_table()
                 w_copy.wait()
                 cw_copy.wait()
         from_sibling(0)
@@ -280,6 +290,7 @@
         score(1, 1)
     else:
         prepare_pick()
+        make_table()
         own_copy.wait()
         from_row(0)
 
@@ -344,12 +355,12 @@
     slots = max(32, 2 * rows * owners // n)
     assert slots == 32 and rows == 64 and 2 * labels * owners == 128 and n % 8 == 0
     vmem = pl.BlockSpec(memory_space=pltpu.VMEM)
-    hbm = pl.BlockSpec(memory_space=pl.ANY)
+    hbm = pl.BlockSpec(memory_space=pltpu.HBM)
     dma = pltpu.SemaphoreType.DMA
     return pl.pallas_call(
         functools.partial(kernel, n, chips_along_x(n), slots),
         out_shape=jax.ShapeDtypeStruct((rows, 2 * labels * owners), jnp.float32),
-        in_specs=[hbm, vmem, vmem, hbm, vmem, hbm, vmem],
+        in_specs=[hbm] * 7,
         out_specs=vmem,
         scratch_shapes=[
             pltpu.VMEM((n, rows, features), queries.dtype),
@@ -360,11 +371,16 @@
             pltpu.VMEM((n, 8, 128), jnp.float32),
             pltpu.VMEM((n, 8, 128), jnp.float32),
             pltpu.VMEM((owners, rows, n * slots), jnp.bfloat16),
+            pltpu.VMEM((owners, rows), jnp.int32),
+            pltpu.VMEM((2 * owners, rows), jnp.int32),
+            pltpu.VMEM((labels, clusters), jnp.float32),
+            pltpu.VMEM((1, clusters), jnp.int32),
+            pltpu.VMEM((4 * labels, clusters), jnp.bfloat16),
             dma((n - 1,)), dma((n - 1,)), dma((n,)), dma((n,)), dma((n,)), dma((n,)),
-            dma, dma, dma,
+            dma((7,)),
         ],
         compiler_params=pltpu.CompilerParams(
-            collective_id=0, has_side_effects=True, vmem_limit_bytes=48 * 2**20
+            collective_id=0, has_side_effects=True, vmem_limit_bytes=56 * 2**20
         ),
     )(
         queries,

time: 36.4 us -> 31.4 us (0.86)
  local copies, waits for them, and re-layouts: 7.04 us -> 1.38 us
  Pallas kernels: 29 us -> 29.8 us
    unnamed x15 -> x1, local copies, waits for them, and re-layouts: 7.04 us -> 1.38 us
    pallas_call x1, Pallas kernels: 29 us -> 29.8 us  [on_device(): pl.pallas_call(functools.partial(kernel, n, chips_along_x(n), slots), out...]
where the time goes in v2:
time: 31.4 us; the launch traced here: 31.2 us
  Pallas kernels  29.8 us (95%)
  local copies, waits for them, and re-layouts  1.38 us (4%)
    pallas_call x1, Pallas kernels, on_device(): pl.pallas_call(functools.partial(kernel, n, chips_along_x(n), slots), out...  29.8 us
    unnamed x1, local copies, waits for them, and re-layouts  1.38 us

profile of v2, /device:TPU:0, one launch (start us, length us, event | category | flops | bytes accessed | tf_op | source)
XLA Modules:
  0.0 31.2 jit_solution(5651494897551928083)
XLA Ops:
  0.0 29.8 %shard_map.73 = f32[64,128]{1,0:T(8,128)} custom-call(bf16[64,768]{1,0:T(8,128)(2,1)} %q_hbm.1, s32[4,64]{1,0:T(4,128)} %bitcast.8, s32[8,64]{1,0:T(8,128)} %bitcast.7, bf16[2048,768]{1,0:T(8,128)(2,1)} %bitcast.5, f32[16,128]{1,0:T(8,128)} %bitcast.6, bf16[128,768]{1,0:T(8,128)(2,1)} %cw_hbm.1, s32[1,128]{1,0:T(1,128)} %bitcast.9), custom_call_target="tpu_custom_call" | custom-call | tf_op jit(solution)/shard_map/pallas_call | solution.py:360
  29.8 1.4 %copy.9 = f32[64,128]{1,0:T(8,128)} copy(f32[64,128]{1,0:T(8,128)} %shard_map.73) | data formatting | bytes 65536

commit v3 on v2

--- a/solution.py
+++ b/solution.py
@@ -29,11 +29,11 @@
 
 
 def kernel(
-    n, nx, slots,
+    n, nx, slots, pieces,
     q_hbm, owner_hbm, local_hbm, w_hbm, bias_hbm, cw_hbm, size_hbm,
     out_ref,
     gath, idx, w, cw, xc, stage, ret, pick, owner_ref, local_ref, bias_ref, size_ref, table,
-    send_q, send_i, recv_q, recv_i, send_r, recv_r, load_sem,
+    send_q, send_i, recv_i, send_r, recv_r, recv_z, recv_x, recv_c, recv_zi, recv_xi, load_sem,
 ):
     rows, features = q_hbm.shape
     clusters = cw_hbm.shape[0]
@@ -41,6 +41,7 @@
     pair = 2 * labels
     nz = n // (2 * nx)
     quads_per_plane = nx // 2
+    piece = rows // pieces
     me = lax.axis_index("wide")
     core = lax.rem(me, 2)
     x = lax.rem(me // 2, nx)
@@ -50,16 +51,21 @@
         return (z_ * nx + x_) * 2 + core_
 
     def plane(k):
-        return lax.rem(z + k, nz)
+        other, bit = 0, 1
+        while bit < nz:
+            mine, turned = lax.rem(z // bit, 2), k // bit % 2
+            other = other + bit * (mine + turned - 2 * mine * turned)
+            bit *= 2
+        return other
 
     barrier = pltpu.get_barrier_semaphore()
 
-    def greet(step):
-        pl.semaphore_signal(
-            barrier, inc=1, device_id={"wide": lax.rem(me + step + 1, n)}, device_id_type=MESH
-        )
-
-    loop(n - 1, greet)
+    def greet(target):
+        pl.semaphore_signal(barrier, inc=1, device_id={"wide": target}, device_id_type=MESH)
+
+    loop(nz - 1, lambda step: greet(index_of(plane(step + 1), x, core)))
+    loop(nx - 1, lambda step: greet(index_of(z, lax.rem(x + 1 + step, nx), core)))
+    greet(index_of(z, x, 1 - core))
 
     loads = [
         pltpu.make_async_copy(source, target, load_sem.at[i])
@@ -79,62 +85,108 @@
     named = jnp.concatenate(
         [owner[k // 2:k // 2 + 1] * clusters + local[k:k + 1] for k in range(local.shape[0])], axis=0
     )
-    idx[me] = jnp.concatenate([named, named], axis=1)
-
-    pl.semaphore_wait(barrier, n - 1)
-
-    def send_chunk(source, number, slot, target):
+    half_beams = local.shape[0] // 2
+    idx[me] = jnp.concatenate([named[:half_beams], named[half_beams:]], axis=1)
+
+    own_copy.wait()
+    pl.semaphore_wait(barrier, nz + nx - 1)
+
+    def send_idx(number, recv, target):
         pltpu.make_async_remote_copy(
-            src_ref=idx.at[number], dst_ref=idx.at[number],
-            send_sem=send_i.at[slot], recv_sem=recv_i.at[number],
+            src_ref=idx.at[number], dst_ref=idx.at[number], send_sem=send_i, recv_sem=recv,
             device_id={"wide": target}, device_id_type=MESH,
         ).start()
+
+    def wait_one(ref, sem):
+        pltpu.make_async_copy(ref, ref, sem).wait()
+
+    def part(number, p):
+        return gath.at[number, pl.ds(p * piece, piece)]
+
+    def send(source, number, p, recv, target):
         pltpu.make_async_remote_copy(
-            src_ref=source, dst_ref=gath.at[number],
-            send_sem=send_q.at[slot], recv_sem=recv_q.at[number],
+            src_ref=source, dst_ref=part(number, p), send_sem=send_q, recv_sem=recv,
             device_id={"wide": target}, device_id_type=MESH,
         ).start()
 
-    def wait_chunk(number):
-        pltpu.make_async_copy(idx.at[number], idx.at[number], recv_i.at[number]).wait()
-        pltpu.make_async_copy(gath.at[number], gath.at[number], recv_q.at[number]).wait()
-
-    def to_column(step):
-        send_chunk(q_hbm, me, step, index_of(lax.rem(z + nz - 1 - step, nz), x, core))
-
-    x_base = nz - 1
-    c_base = x_base + nz * (nx - 1)
-
-    def to_row(source, number, k):
+    def to_column(k, p):
+        if p == 0:
+            send_idx(me, recv_zi.at[k], index_of(plane(k), x, core))
+        send(own_part(p), me, p, recv_z.at[k * pieces + p], index_of(plane(k), x, core))
+
+    def to_row(source, number, k, p):
         def one(step):
             other = lax.rem(x + 1 + step, nx)
-            send_chunk(source, number, x_base + k * (nx - 1) + step, index_of(z, other, core))
+            if p == 0:
+                send_idx(number, recv_xi.at[k * (nx - 1) + step], index_of(z, other, core))
+            send(source, number, p, recv_x.at[(k * (nx - 1) + step) * pieces + p], index_of(z, other, core))
         loop(nx - 1, one)
 
-    def to_sibling(source, number, k, step):
-        send_chunk(source, number, c_base + k * nx + step, index_of(z, x, 1 - core))
-
-    to_row(q_hbm, me, 0)
-    loop(nz - 1, to_column)
-    to_sibling(q_hbm, me, 0, 0)
-
-    def from_column(k):
+    def to_sibling(source, number, k, p):
+        if p == 0:
+            send_idx(number, recv_i.at[k], index_of(z, x, 1 - core))
+        send(source, number, p, recv_c.at[k], index_of(z, x, 1 - core))
+
+    def own_part(p):
+        return part(me, p)
+
+    def from_column(k, pass_on=False):
         number = index_of(plane(k), x, core)
-        wait_chunk(number)
-        to_row(gath.at[number], number, k)
-        to_sibling(gath.at[number], number, k, 0)
+        wait_one(idx.at[number], recv_zi.at[k])
+        for p in range(pieces):
+            pltpu.make_async_copy(part(number, p), part(number, p), recv_z.at[k * pieces + p]).wait()
+            to_row(part(number, p), number, k, p)
+            if pass_on:
+                @pl.when(middle)
+                def _():
+                    if p == 0:
+                        send_idx(number, recv_zi.at[2], index_of(plane(1), x, core))
+                    send(part(number, p), number, p, recv_z.at[2 * pieces + p], index_of(plane(1), x, core))
+            to_sibling(part(number, p), number, k, p)
 
     def from_row(k):
         def one(step):
-            number = index_of(plane(k), lax.rem(x + 1 + step, nx), core)
-            wait_chunk(number)
-            to_sibling(gath.at[number], number, k, 1 + step)
+            number = index_of(plane(k), lax.rem(x + nx - 1 - step, nx), core)
+            wait_one(idx.at[number], recv_xi.at[k * (nx - 1) + step])
+            for p in range(pieces):
+                recv = recv_x.at[(k * (nx - 1) + step) * pieces + p]
+                pltpu.make_async_copy(part(number, p), part(number, p), recv).wait()
+                to_sibling(part(number, p), number, k, p)
         loop(nx - 1, one)
 
     def from_sibling(k):
-        def one(step):
-            wait_chunk(index_of(plane(k), step, 1 - core))
-        loop(nx, one)
+        some = gath.at[pl.ds(0, nx)]
+        pltpu.make_async_copy(some, some, recv_c.at[k]).wait()
+
+    relayed = n <= SMALL and nx == 2 and nz == 4
+    middle = (z == 1) | (z == 2)
+
+    def relay_order(step):
+        return jnp.where(middle, (3, 1, 2)[step], step + 1)
+
+    order = [0] + [relay_order(step) for step in range(3)]
+
+    if not relayed:
+        for p in range(pieces):
+            to_row(own_part(p), me, 0, p)
+    if relayed:
+        for p in range(pieces):
+            to_column(1, p)
+            to_row(own_part(p), me, 0, p)
+
+            @pl.when(middle)
+            def _():
+                to_column(3, p)
+
+        @pl.when(jnp.logical_not(middle))
+        def _():
+            for k in (2, 3):
+                for p in range(pieces):
+                    to_column(k, p)
+    else:
+        loop(nz - 1, lambda step: [to_column(step + 1, p) for p in range(pieces)])
+    for p in range(pieces):
+        to_sibling(own_part(p), me, 0, p)
 
     def make_table():
         size_copy.wait()
@@ -174,19 +226,25 @@
     width = QUAD * rows
 
     def quad_number(position):
+        if relayed:
+            return plane(order[position])
         return plane(position // quads_per_plane) * quads_per_plane + position % quads_per_plane
 
-    def compact(position, half, slot_of):
+    def choose(position):
         first = QUAD * quad_number(position)
-        lane = lax.broadcasted_iota(jnp.int32, (8, 128), 1)
-        row = lax.broadcasted_iota(jnp.int32, (8, 128), 0)
+        lane = lax.broadcasted_iota(jnp.int32, (half_beams, 128), 1)
+        row = lax.broadcasted_iota(jnp.int32, (2 * half_beams, 128), 0)
         parts = []
         for p in range(QUAD // 2):
-            ids = jnp.where(lane < rows, idx[first + 2 * p], idx[first + 2 * p + 1])
+            left, right = idx[first + 2 * p], idx[first + 2 * p + 1]
+            ids = jnp.concatenate([
+                jnp.where(lane < rows, left, pltpu.roll(right, rows, axis=1)),
+                jnp.where(lane < rows, pltpu.roll(left, rows, axis=1), right),
+            ], axis=0)
             ids = ids - me * clusters
             inside = (ids >= 0) & (ids < clusters)
             value = jnp.where(inside, ids, 0).astype(jnp.float32)
-            even = row % 2 == 0
+            even = lax.rem(row, 2) == 0
             c0 = jnp.sum(jnp.where(even, value, 0.0), axis=0, keepdims=True)
             c1 = jnp.sum(jnp.where(even, 0.0, value), axis=0, keepdims=True)
             hit = jnp.sum(jnp.where(even & inside, 1.0, 0.0), axis=0, keepdims=True)
@@ -207,16 +265,16 @@
         row = lax.broadcasted_iota(jnp.int32, (8, width), 0)
         both = jnp.where(row == 0, c0, jnp.where(row == 1, c1, 0.0)).astype(jnp.bfloat16)
         chosen = lax.dot_general(both, taken, NT, preferred_element_type=jnp.float32)
-        embedded = gath[pl.ds(first, QUAD)].reshape(width, features)
-        packed = jnp.dot(taken, embedded, preferred_element_type=jnp.float32)
-        xc[slot_of, half * QUAD * slots:(half + 1) * QUAD * slots] = packed.astype(jnp.bfloat16)
-        return chosen[0:1], chosen[1:2]
-
-    def score(batch, slot_of):
-        chosen = [compact(2 * batch + half, half, slot_of) for half in range(2)]
-        ids = [jnp.concatenate(v, axis=1).astype(jnp.int32) for v in zip(*chosen)]
-        lanes = 2 * QUAD * slots
-        x_rows = xc[slot_of]
+        return first, taken, chosen[0:1], chosen[1:2]
+
+    def score(picks, slot_of):
+        lanes = QUAD * slots * len(picks)
+        for place, (first, taken, _, _) in enumerate(picks):
+            embedded = gath[pl.ds(first, QUAD)].reshape(width, features)
+            packed = jnp.dot(taken, embedded, preferred_element_type=jnp.float32)
+            xc[slot_of, place * QUAD * slots:(place + 1) * QUAD * slots] = packed.astype(jnp.bfloat16)
+        ids = [jnp.concatenate([v[2 + k] for v in picks], axis=1).astype(jnp.int32) for k in range(2)]
+        x_rows = xc[slot_of, :lanes]
         wide_ids = [jnp.broadcast_to(v, (labels, lanes)) for v in ids]
         logit = [jnp.zeros((labels, lanes), jnp.float32) for _ in ids]
         step = min(16, clusters)
@@ -242,8 +300,7 @@
             scores.append(jnp.where(slot < used, value, 0.0))
         scores = jnp.concatenate(scores, axis=0)
         lane = lax.broadcasted_iota(jnp.int32, (8, 128), 1)
-        for half in range(2):
-            first = QUAD * quad_number(2 * batch + half)
+        for half, (first, _, _, _) in enumerate(picks):
             for t in range(QUAD):
                 tile = jnp.zeros((8, 128), jnp.float32)
                 for g in range(QUAD):
@@ -253,8 +310,7 @@
                         part = pltpu.roll(part, shift, axis=1)
                     tile = jnp.where(lane // slots == g, part, tile)
                 stage[first + t] = tile
-        for half in range(2):
-            first = QUAD * quad_number(2 * batch + half)
+        for first, _, _, _ in picks:
             for t in range(QUAD):
                 target = first + t
 
@@ -262,7 +318,7 @@
                 def _():
                     pltpu.make_async_remote_copy(
                         src_ref=stage.at[target], dst_ref=ret.at[me],
-                        send_sem=send_r.at[target], recv_sem=recv_r.at[me],
+                        send_sem=send_r, recv_sem=recv_r,
                         device_id={"wide": target}, device_id_type=MESH,
                     ).start()
 
@@ -271,27 +327,35 @@
                     ret[me] = stage[me]
 
     batches = n // (2 * QUAD)
-    if n <= SMALL and nx == 2:
-        own_copy.wait()
-        for k in range(1, nz):
-            from_column(k)
-            from_row(k - 1)
-            if k == 1:
-                prepare_pick()
-                make_table()
-                w_copy.wait()
-                cw_copy.wait()
-        from_sibling(0)
-        from_sibling(1)
-        score(0, 0)
-        from_row(nz - 1)
-        from_sibling(2)
-        from_sibling(3)
-        score(1, 1)
+
+    def wait_idx(k):
+        wait_one(idx.at[pl.ds(0, nx)], recv_i.at[k])
+
+    prepare_pick()
+    make_table()
+    if relayed:
+        from_column(order[1], pass_on=True)
+        from_row(order[0])
+        from_column(order[2])
+        from_row(order[1])
+        from_column(order[3])
+        from_row(order[2])
+        from_sibling(order[0])
+        from_sibling(order[1])
+        w_copy.wait()
+        cw_copy.wait()
+        wait_idx(order[0])
+        wait_idx(order[1])
+        score([choose(0), choose(1)], 0)
+        wait_idx(order[2])
+        picks = [choose(2)]
+        from_row(order[3])
+        wait_idx(order[3])
+        picks.append(choose(3))
+        from_sibling(order[2])
+        from_sibling(order[3])
+        score(picks, 1)
     else:
-        prepare_pick()
-        make_table()
-        own_copy.wait()
         from_row(0)
 
         def relay(step):
@@ -302,13 +366,11 @@
         loop(nz, from_sibling)
         w_copy.wait()
         cw_copy.wait()
-        lax.fori_loop(0, batches, lambda b, carry: (score(b, 0), carry)[1], 0)
-
-    def wait_return(step):
-        source = lax.rem(me + 1 + step, n)
-        pltpu.make_async_copy(ret.at[source], ret.at[source], recv_r.at[source]).wait()
-
-    loop(n - 1, wait_return)
+        loop(nz, wait_idx)
+        lax.fori_loop(0, batches, lambda b, carry: (score([choose(2 * b), choose(2 * b + 1)], 0), carry)[1], 0)
+
+    most = pl.ds(0, n - 1)
+    pltpu.make_async_copy(ret.at[most], ret.at[most], recv_r).wait()
 
     lane = lax.broadcasted_iota(jnp.int32, (8, 128), 1)
     columns = []
@@ -336,16 +398,8 @@
             result += lax.dot_general(pick[k], spread, NT, preferred_element_type=jnp.float32)
     out_ref[...] = result
 
-    def wait_sent(step):
-        pltpu.make_async_copy(idx.at[0], idx.at[0], send_i.at[step]).wait()
-        pltpu.make_async_copy(gath.at[0], gath.at[0], send_q.at[step]).wait()
-
-    def wait_returned(step):
-        target = lax.rem(me + 1 + step, n)
-        pltpu.make_async_copy(stage.at[target], stage.at[target], send_r.at[target]).wait()
-
-    loop(n - 1, wait_sent)
-    loop(n - 1, wait_returned)
+    for sent, sem in ((idx, send_i), (gath, send_q), (stage, send_r)):
+        pltpu.make_async_copy(sent.at[most], sent.at[most], sem).wait()
 
 
 def on_device(n, queries, beam_owner, beam_local, leaf_weight, leaf_bias, cluster_weight, block_size):
@@ -354,17 +408,19 @@
     clusters, labels, _ = leaf_weight.shape
     slots = max(32, 2 * rows * owners // n)
     assert slots == 32 and rows == 64 and 2 * labels * owners == 128 and n % 8 == 0
+    nx = chips_along_x(n)
+    nz = n // (2 * nx)
     vmem = pl.BlockSpec(memory_space=pltpu.VMEM)
     hbm = pl.BlockSpec(memory_space=pltpu.HBM)
     dma = pltpu.SemaphoreType.DMA
     return pl.pallas_call(
-        functools.partial(kernel, n, chips_along_x(n), slots),
+        functools.partial(kernel, n, nx, slots, 4),
         out_shape=jax.ShapeDtypeStruct((rows, 2 * labels * owners), jnp.float32),
         in_specs=[hbm] * 7,
         out_specs=vmem,
         scratch_shapes=[
             pltpu.VMEM((n, rows, features), queries.dtype),
-            pltpu.VMEM((n, 8, 128), jnp.int32),
+            pltpu.VMEM((n, owners, 128), jnp.int32),
             pltpu.VMEM((clusters * labels, features), leaf_weight.dtype),
             pltpu.VMEM((clusters, features), cluster_weight.dtype),
             pltpu.VMEM((2, 2 * QUAD * slots, features), jnp.bfloat16),
@@ -376,8 +432,8 @@
             pltpu.VMEM((labels, clusters), jnp.float32),
             pltpu.VMEM((1, clusters), jnp.int32),
             pltpu.VMEM((4 * labels, clusters), jnp.bfloat16),
-            dma((n - 1,)), dma((n - 1,)), dma((n,)), dma((n,)), dma((n,)), dma((n,)),
-            dma((7,)),
+            dma, dma, dma((nz,)), dma, dma,
+            dma((nz * 4,)), dma((nz * (nx - 1) * 4,)), dma((nz,)), dma((nz,)), dma((nz * (nx - 1),)), dma((7,)),
         ],
         compiler_params=pltpu.CompilerParams(
             collective_id=0, has_side_effects=True, vmem_limit_bytes=56 * 2**20

time: 31.4 us -> 27.1 us (0.86)
  Pallas kernels: 29.8 us -> 25.5 us
    pallas_call x1, Pallas kernels: 29.8 us -> 25.5 us  [on_device(): pl.pallas_call(functools.partial(kernel, n, nx, slots, 4), out_shape=jax....]
where the time goes in v3:
time: 27.1 us; the launch traced here: 26.9 us
  Pallas kernels  25.5 us (94%)
  local copies, waits for them, and re-layouts  1.38 us (5%)
    pallas_call x1, Pallas kernels, on_device(): pl.pallas_call(functools.partial(kernel, n, nx, slots, 4), out_shape=jax....  25.5 us
    unnamed x1, local copies, waits for them, and re-layouts  1.38 us

profile of v3, /device:TPU:0, one launch (start us, length us, event | category | flops | bytes accessed | tf_op | source)
XLA Modules:
  0.0 26.9 jit_solution(17633251822725138820)
XLA Ops:
  0.0 25.5 %shard_map.73 = f32[64,128]{1,0:T(8,128)} custom-call(bf16[64,768]{1,0:T(8,128)(2,1)} %q_hbm.1, s32[4,64]{1,0:T(4,128)} %bitcast.8, s32[8,64]{1,0:T(8,128)} %bitcast.7, bf16[2048,768]{1,0:T(8,128)(2,1)} %bitcast.5, f32[16,128]{1,0:T(8,128)} %bitcast.6, bf16[128,768]{1,0:T(8,128)(2,1)} %cw_hbm.1, s32[1,128]{1,0:T(1,128)} %bitcast.9), custom_call_target="tpu_custom_call" | custom-call | tf_op jit(solution)/shard_map/pallas_call | solution.py:416
  25.5 1.4 %copy.9 = f32[64,128]{1,0:T(8,128)} copy(f32[64,128]{1,0:T(8,128)} %shard_map.73) | data formatting | bytes 65536

commit v4 on v3

--- a/solution.py
+++ b/solution.py
@@ -127,6 +127,13 @@
             send_idx(number, recv_i.at[k], index_of(z, x, 1 - core))
         send(source, number, p, recv_c.at[k], index_of(z, x, 1 - core))
 
+    def all_to_sibling(number, k):
+        send_idx(number, recv_i.at[k], index_of(z, x, 1 - core))
+        pltpu.make_async_remote_copy(
+            src_ref=gath.at[number], dst_ref=gath.at[number], send_sem=send_q, recv_sem=recv_c.at[k],
+            device_id={"wide": index_of(z, x, 1 - core)}, device_id_type=MESH,
+        ).start()
+
     def own_part(p):
         return part(me, p)
 
@@ -142,16 +149,19 @@
                     if p == 0:
                         send_idx(number, recv_zi.at[2], index_of(plane(1), x, core))
                     send(part(number, p), number, p, recv_z.at[2 * pieces + p], index_of(plane(1), x, core))
-            to_sibling(part(number, p), number, k, p)
-
-    def from_row(k):
+        all_to_sibling(number, k)
+
+    def from_row(k, split=False):
         def one(step):
             number = index_of(plane(k), lax.rem(x + nx - 1 - step, nx), core)
             wait_one(idx.at[number], recv_xi.at[k * (nx - 1) + step])
             for p in range(pieces):
                 recv = recv_x.at[(k * (nx - 1) + step) * pieces + p]
                 pltpu.make_async_copy(part(number, p), part(number, p), recv).wait()
-                to_sibling(part(number, p), number, k, p)
+                if split:
+                    to_sibling(part(number, p), number, k, p)
+            if not split:
+                all_to_sibling(number, k)
         loop(nx - 1, one)
 
     def from_sibling(k):
@@ -185,8 +195,7 @@
                     to_column(k, p)
     else:
         loop(nz - 1, lambda step: [to_column(step + 1, p) for p in range(pieces)])
-    for p in range(pieces):
-        to_sibling(own_part(p), me, 0, p)
+    all_to_sibling(me, 0)
 
     def make_table():
         size_copy.wait()
@@ -267,12 +276,16 @@
         chosen = lax.dot_general(both, taken, NT, preferred_element_type=jnp.float32)
         return first, taken, chosen[0:1], chosen[1:2]
 
-    def score(picks, slot_of):
+    def pack(pick, slot_of, place):
+        first, taken, _, _ = pick
+        embedded = gath[pl.ds(first, QUAD)].reshape(width, features)
+        packed = jnp.dot(taken, embedded, preferred_element_type=jnp.float32)
+        xc[slot_of, place * QUAD * slots:(place + 1) * QUAD * slots] = packed.astype(jnp.bfloat16)
+
+    def score(picks, slot_of, ready=0):
         lanes = QUAD * slots * len(picks)
-        for place, (first, taken, _, _) in enumerate(picks):
-            embedded = gath[pl.ds(first, QUAD)].reshape(width, features)
-            packed = jnp.dot(taken, embedded, preferred_element_type=jnp.float32)
-            xc[slot_of, place * QUAD * slots:(place + 1) * QUAD * slots] = packed.astype(jnp.bfloat16)
+        for place in range(ready, len(picks)):
+            pack(picks[place], slot_of, place)
         ids = [jnp.concatenate([v[2 + k] for v in picks], axis=1).astype(jnp.int32) for k in range(2)]
         x_rows = xc[slot_of, :lanes]
         wide_ids = [jnp.broadcast_to(v, (labels, lanes)) for v in ids]
@@ -310,7 +323,7 @@
                         part = pltpu.roll(part, shift, axis=1)
                     tile = jnp.where(lane // slots == g, part, tile)
                 stage[first + t] = tile
-        for first, _, _, _ in picks:
+        for first, _, _, _ in picks[::-1]:
             for t in range(QUAD):
                 target = first + t
 
@@ -349,12 +362,13 @@
         score([choose(0), choose(1)], 0)
         wait_idx(order[2])
         picks = [choose(2)]
-        from_row(order[3])
+        from_row(order[3], split=True)
         wait_idx(order[3])
         picks.append(choose(3))
         from_sibling(order[2])
+        pack(picks[0], 1, 0)
         from_sibling(order[3])
-        score(picks, 1)
+        score(picks, 1, ready=1)
     else:
         from_row(0)
 

time: 27.1 us -> 27.1 us (level)
  no operation moved by 1% of the time
where the time goes in v4:
time: 27.1 us; the launch traced here: 26.9 us
  Pallas kernels  25.5 us (94%)
  local copies, waits for them, and re-layouts  1.38 us (5%)
    pallas_call x1, Pallas kernels, on_device(): pl.pallas_call(functools.partial(kernel, n, nx, slots, 4), out_shape=jax....  25.5 us
    unnamed x1, local copies, waits for them, and re-layouts  1.38 us

profile of v4, /device:TPU:0, one launch (start us, length us, event | category | flops | bytes accessed | tf_op | source)
XLA Modules:
  0.0 26.9 jit_solution(3891904537053328880)
XLA Ops:
  0.0 25.5 %shard_map.73 = f32[64,128]{1,0:T(8,128)} custom-call(bf16[64,768]{1,0:T(8,128)(2,1)} %q_hbm.1, s32[4,64]{1,0:T(4,128)} %bitcast.8, s32[8,64]{1,0:T(8,128)} %bitcast.7, bf16[2048,768]{1,0:T(8,128)(2,1)} %bitcast.5, f32[16,128]{1,0:T(8,128)} %bitcast.6, bf16[128,768]{1,0:T(8,128)(2,1)} %cw_hbm.1, s32[1,128]{1,0:T(1,128)} %bitcast.9), custom_call_target="tpu_custom_call" | custom-call | tf_op jit(solution)/shard_map/pallas_call | solution.py:430
  25.5 1.4 %copy.9 = f32[64,128]{1,0:T(8,128)} copy(f32[64,128]{1,0:T(8,128)} %shard_map.73) | data formatting | bytes 65536
